TPU v7x, 256 devices: a whole 4x4x8 slice. The times are simulated.
256 devices in a mesh: mp: 2 (over y_lo), dp: 32 (over z, x), vocab: 4 (over y_hi, core).
Axes of the slice: x: 4, y: 4 (y_hi: 2, y_lo: 2; y = y_hi * 2 + y_lo), z: 8, core: 2. Of those that a mesh axis runs over, the one named last changes fastest.
Arguments:
- hidden_states: bfloat16 [2, 1024, 4096], P('mp', 'dp'), may hold values from -700 to 700
- head_weight: bfloat16 [2, 4096, 65536], P('mp', None, ('dp', 'vocab')), may hold values from -1 to 1
- targets: int32 [1024], replicated, may hold values from 0 to 65535
- train_step: int32 [1], replicated, may hold values from 0 to 999
Outputs:
- grad_hidden: float32 [2, 1024, 4096], P('mp', 'dp', 'vocab')
- grad_head: float32 [2, 4096, 65536], P('mp', None, ('dp', 'vocab'))
All inputs are finite; a program needn't handle non-finite values.
Results may differ from a plain program's by a relative error of at most 0.0029.
Values may be sent and summed in bfloat16 or wider, within the bound.
No kernel may reach another device: no remote copies, remote signals or barrier semaphores. Data moves between devices by JAX's collectives and lax.ppermute only.
A program may use at most 128 MiB of HBM per device.

v0:
```python
import jax
import jax.numpy as jnp
from jax import lax
from jax.sharding import PartitionSpec as P

WARMUP = 1000


def partner(value, axis, distance):
    mask = 2**distance
    pairs = [(source, source ^ mask) for source in range(lax.axis_size(axis))]
    return lax.ppermute(value, axis, pairs)


def row_log_norm(values):
    local_peak = jnp.max(values, axis=-1)
    row_max = lax.pmax(local_peak, ("dp", "vocab"))
    row_sum = lax.psum(jnp.sum(jnp.exp(values - row_max[..., None]), axis=-1), ("dp", "vocab"))
    return row_max + jnp.log(row_sum)


def per_device(hidden_states, head_weight, targets, train_step):
    gathered = lax.all_gather(hidden_states, "dp", axis=1, tiled=True)[0]
    weight = head_weight[0]
    columns_dev = weight.shape[1]
    offset = lax.axis_index(("dp", "vocab")) * columns_dev
    share = 0.5 * jnp.minimum(train_step[0].astype(jnp.float32) / WARMUP, 1.0)
    logits = jnp.dot(gathered, weight, preferred_element_type=jnp.float32)
    own_logp = logits - row_log_norm(logits)[:, None]
    partner_logp = partner(own_logp, "mp", 0)
    own_probs = jnp.exp(own_logp)
    partner_probs = jnp.exp(partner_logp)
    column_ids = offset + lax.iota(jnp.int32, columns_dev)
    onehot = (column_ids[None, :] == targets[:, None]).astype(jnp.float32)
    logit_grad = ((1.0 + share) * own_probs - onehot - share * partner_probs).astype(jnp.bfloat16)
    grad_head = lax.dot_general(
        gathered, logit_grad, (((0,), (0,)), ((), ())), preferred_element_type=jnp.float32
    )
    row_part = lax.psum_scatter(
        lax.dot_general(
            logit_grad, weight, (((1,), (1,)), ((), ())), preferred_element_type=jnp.float32
        ),
        "dp",
        scatter_dimension=0,
        tiled=True,
    )
    result = lax.psum_scatter(row_part, "vocab", scatter_dimension=1, tiled=True)
    return (result[None], grad_head[None])


def solution(mesh):
    placed = (P("mp", "dp", None), P("mp", None, ("dp", "vocab")), P(), P())
    return jax.shard_map(
        per_device,
        mesh=mesh,
        in_specs=placed,
        out_specs=(P("mp", "dp", "vocab"), P("mp", None, ("dp", "vocab"))),
        check_vma=False,
    )
```

profile of v0, /device:TPU:1, one launch (start us, length us, event | category | flops | bytes accessed | tf_op | source)
XLA Modules:
  0.0 1113.1 jit_solution(17014889742502147903)
XLA Ops:
  7.2 0.0 all-gather.2.cloned.1.call-start
  7.2 0.7 all-gather.2.cloned.1.call-update
  7.9 0.0 reduce-scatter.3.cloned.1.call-start
  7.9 104.4 %all-gather.2.cloned.1.call-done = bf16[1,1024,4096]{2,1,0:T(8,128)(2,1)} async-done(((bf16[1,32,4096]{2,1,0:T(8,128)(2,1)}), bf16[1,1024,4096]{2,1,0:T(8,128)(2,1)}) %all-gather.2.cloned.1.call-update) | async-done | bytes 8388624 | tf_op jit(solution)/shard_map/all_gather | solution.py:23
  112.3 8.3 fusion.10
  120.6 324.2 %pmax.7 = f32[1024]{0:T(1024)S(1)} all-reduce(f32[1024]{0:T(1024)S(1)} %get-tuple-element.4), channel_id=1, replica_groups=mesh['mp'=2,'dp'=32,'vocab'=4] {'dp','vocab'}, use_global_device_ids=true, to_apply=%region_1.0 | all-reduce | flops 1024 | bytes 8192 | tf_op jit(solution)/shard_map/pmax | solution.py:17
  444.8 0.3 exponential_reduce_fusion
  445.1 326.8 %psum.7 = f32[1024]{0:T(1024)S(1)} all-reduce(f32[1024]{0:T(1024)S(1)} %exponential_reduce_fusion), channel_id=1, replica_groups=mesh['mp'=2,'dp'=32,'vocab'=4] {'dp','vocab'}, use_global_device_ids=true, to_apply=%region_3.0 | all-reduce | flops 1024 | bytes 8192 | tf_op jit(solution)/shard_map/psum | solution.py:18
  771.9 0.0 copy-start
  771.9 1.5 broadcast_subtract_fusion
  773.5 0.3 collective-permute-start
  774.5 0.0 copy-start.1
  774.5 45.7 %collective-permute-done = f32[1024,512]{0,1:T(8,128)} collective-permute-done((f32[1024,512]{0,1:T(8,128)}, f32[1024,512]{0,1:T(8,128)}, u32[]{:S(2)}, u32[]{:S(2)}) %collective-permute-start) | collective-permute-done | bytes 2097184 | tf_op jit(solution)/shard_map/ppermute | solution.py:12
  820.2 0.0 copy-done
  820.2 2.4 subtract_convert_fusion
  822.6 0.0 copy-done.1
  822.6 8.1 fusion.7
  830.7 0.0 reduce-scatter.3.cloned.1.call-update
  830.8 0.0 reduce-scatter.5.cloned.1.call-start
  830.8 236.0 %reduce-scatter.3.cloned.1.call-done = f32[32,4096]{1,0:T(8,128)} async-done(((f32[1024,4096]{1,0:T(8,128)}), f32[32,4096]{1,0:T(8,128)}) %reduce-scatter.3.cloned.1.call-update) | async-done | bytes 524304 | tf_op jit(solution)/shard_map/reduce_scatter | solution.py:39
  1066.8 0.0 reduce-scatter.5.cloned.1.call-update
  1066.9 10.1 fusion.4
  1076.9 9.0 copy.6
  1085.9 20.7 %reduce-scatter.5.cloned.1.call-done = f32[32,1024]{1,0:T(8,128)} async-done(((f32[32,4096]{1,0:T(8,128)}), f32[32,1024]{1,0:T(8,128)}) %reduce-scatter.5.cloned.1.call-update) | async-done | bytes 131088 | tf_op jit(solution)/shard_map/reduce_scatter | solution.py:47
  (2 shorter events, 0.0 us)
Async XLA Ops:
  7.2 105.2 %all-gather.2.cloned.1.call-start = ((), (), s32[]{:S(2)}) async-start(), calls=%async_computation.2 | async-start | bytes 8650752 | tf_op jit(solution)/shard_map/all_gather | solution.py:23
  7.9 1058.9 %reduce-scatter.3.cloned.1.call-start = ((), (), s32[]{:S(2)}) async-start(), calls=%async_computation.3 | async-start | bytes 17301504 | tf_op jit(solution)/shard_map/reduce_scatter | solution.py:39
  771.9 48.3 %copy-start = (s32[1024]{0:T(1024)S(1)}, s32[1024]{0:T(1024)}, u32[]{:S(2)}) copy-start(s32[1024]{0:T(1024)} %param.6) | copy-start | bytes 12292
  773.5 46.7 %collective-permute-start = (f32[1024,512]{0,1:T(8,128)}, f32[1024,512]{0,1:T(8,128)}, u32[]{:S(2)}, u32[]{:S(2)}) collective-permute-start(f32[1024,512]{0,1:T(8,128)} %broadcast_subtract_fusion), channel_id=1, source_target_pairs={{0,128},{128,0},{1,129},{129,1},{2,130},{130,2},{3,131},{131,3},{4... | collective-permute-start | bytes 6291464 | tf_op jit(solution)/shard_map/ppermute | solution.py:12
  774.5 48.2 %copy-start.1 = (bf16[1,4096,512]{2,1,0:T(8,128)(2,1)S(1)}, bf16[1,4096,512]{2,1,0:T(8,128)(2,1)}, u32[]{:S(2)}) copy-start(bf16[1,4096,512]{2,1,0:T(8,128)(2,1)} %param.5) | copy-start | bytes 12582916
  830.8 275.8 %reduce-scatter.5.cloned.1.call-start = ((), (), s32[]{:S(2)}) async-start(), calls=%async_computation.4 | async-start | bytes 655360 | tf_op jit(solution)/shard_map/reduce_scatter | solution.py:47
Sparse Core Ops, SparseCore 0:
  10.6 101.6 all-gather.1
  830.9 235.8 reduce-scatter.2
  1070.2 36.3 reduce-scatter.4
where the time goes:
time: 1110 us
  blocking collectives  651 us (59%)
  waiting for transfers between devices  407 us (37%)
  matrix products  26.4 us (2%)
  between operations  14.4 us (1%)
    psum x1, blocking collectives, row_log_norm(): lax.psum(jnp.sum(jnp.exp(values - row_max[..., None]), axis=-1), ('dp', '...  327 us
    pmax x1, blocking collectives, row_log_norm(): row_max = lax.pmax(local_peak, ('dp', 'vocab'))  324 us
    reduce_scatter x1, waiting for transfers between devices, per_device(): lax.psum_scatter(lax.dot_general(logit_grad, weight, (((1,), (1,)), ((),...  236 us
    all_gather x1, waiting for transfers between devices, per_device(): gathered = lax.all_gather(hidden_states, 'dp', axis=1, tiled=True)[0]  104 us
    ppermute x1, waiting for transfers between devices, partner(): return lax.ppermute(value, axis, pairs)  45.7 us
  transfers between devices with their start and end apart: 4, of which 4 were waited for; matrix products, arithmetic and copies ran while one was open for 2% of the time, Pallas kernels for 0%

commit v1 on v0

v1 whole, which is shorter than its diff:
```python
import jax
import jax.numpy as jnp
import numpy as np
from jax import lax
from jax.experimental import pallas as pl
from jax.experimental.pallas import tpu as pltpu
from jax.sharding import PartitionSpec as P

WARMUP = 1000
Z, X = 8, 4
F16 = jnp.float16
F32 = jnp.float32
BF16 = jnp.bfloat16
PROB_SCALE = 2.0**15
GRAD_SCALE = 2.0**14
BIG = 384


def row_tables():
    near, wide = (0, -1, -2, 1), (-3, -4, 2, 3)
    along_z = (0, -1, 1, -2, 2, -3, 3, -4)
    along_x = ((near, 0), (near, -1), (near, 1), (near, -2), (wide, 1), (wide, -1), (wide, 2), (wide, 0))
    table = np.zeros((2, Z * X, 32), np.int32)
    for z in range(Z):
        for x in range(X):
            for i in range(8):
                for j in range(4):
                    at = i * 4 + j
                    table[0, z * X + x, at] = (z + along_z[i]) % Z * X + (x + near[j]) % X
                    offsets, shift = along_x[i]
                    table[1, z * X + x, at] = (z + offsets[j]) % Z * X + (x + shift) % X
    return table, np.argsort(table, axis=-1).astype(np.int32)


def ring(value, axes, step, cores=(0, 1)):
    pairs = []
    for z in range(Z):
        for x in range(X):
            for v in range(4):
                if v % 2 in cores:
                    if axes[v % 2] == "z":
                        to = (z + step) % Z * X + x
                    else:
                        to = z * X + (x + step) % X
                    pairs.append(((z * X + x) * 4 + v, to * 4 + v))
    return lax.ppermute(value, ("dp", "vocab"), pairs)


SMALL, LARGE = ("x", "z"), ("z", "x")


def dp_flip(value, mask):
    return lax.ppermute(value, "dp", [(i, i ^ mask) for i in range(Z * X)])


def vocab_flip(value, mask):
    return lax.ppermute(value, "vocab", [(v, v ^ mask) for v in range(4)])


def partner(value):
    return lax.ppermute(value, "mp", [(0, 1), (1, 0)])


def partner_dp_flip(value, mask):
    n = Z * X
    return lax.ppermute(
        value, ("mp", "dp"), [(m * n + i, (1 - m) * n + (i ^ mask)) for m in range(2) for i in range(n)]
    )


def reordered(table, ref):
    piece = lax.broadcasted_iota(jnp.int32, (1, 128), 1) >> 4
    rows = []
    for r in range(4):
        row = jnp.zeros((1, 128), ref.dtype)
        for c in range(8):
            at = table[r * 8 + c]
            value = pltpu.roll(ref[pl.ds(at >> 3, 1), :], ((c - (at & 7)) & 7) * 16, 1)
            row = jnp.where(piece == c, value, row)
        rows.append(row)
    return rows


def reorder_kernel(table, *refs):
    n = len(refs) // 2
    for source, out in zip(refs[:n], refs[n:]):
        for r, row in enumerate(reordered(table, source)):
            out[r : r + 1, :] = row


def reorder(table, *values):
    smem, vmem = pl.BlockSpec(memory_space=pltpu.SMEM), pl.BlockSpec(memory_space=pltpu.VMEM)
    return pl.pallas_call(
        reorder_kernel,
        in_specs=[smem] + [vmem] * len(values),
        out_shape=tuple(jax.ShapeDtypeStruct((4, 128), v.dtype) for v in values),
    )(table, *values)


def merged(*stats):
    peak = stats[0][0]
    for stat in stats[1:]:
        peak = jnp.maximum(peak, stat[0])
    return peak, sum(stat[1] * jnp.exp(stat[0] - peak) for stat in stats)


def combine(*stats):
    return jnp.stack(merged(*stats))


def factor_kernel(table, share_ref, stat, came, local, p_stat, p_came, own_ref, partner_ref, held):
    share = share_ref[0]
    for out, weight, a, b, peak in (
        (own_ref, 1.0 + share, stat, came, local[...]),
        (partner_ref, share * (1.0 / PROB_SCALE), p_stat, p_came, p_stat[2]),
    ):
        top, total = merged((a[0], a[1]), (b[0], b[1]))
        held[...] = weight * (jnp.exp(peak - top) / total)
        for r, row in enumerate(reordered(table, held)):
            out[r : r + 1, :] = row


def factors(table, share, *stats):
    smem, vmem = pl.BlockSpec(memory_space=pltpu.SMEM), pl.BlockSpec(memory_space=pltpu.VMEM)
    shape = jax.ShapeDtypeStruct((4, 128), F32)
    return pl.pallas_call(
        factor_kernel,
        in_specs=[smem, smem] + [vmem] * 5,
        out_shape=(shape, shape),
        scratch_shapes=[pltpu.VMEM((4, 128), F32)],
    )(table, share.reshape(1), *stats)


def product_kernel(own, other, weight, weight_other, out):
    dims = (((1,), (1,)), ((), ()))
    total = lax.dot_general(own[...], weight[...], dims, preferred_element_type=F32)
    total += lax.dot_general(other[...], weight_other[...], dims, preferred_element_type=F32)
    out[...] = total * GRAD_SCALE


def product(grad, weights, tile=512):
    rows, columns = grad[0].shape
    features = weights[0].shape[0]
    whole = pl.BlockSpec((rows, columns), lambda i: (0, 0))
    part = pl.BlockSpec((tile, columns), lambda i: (i, 0))
    return pl.pallas_call(
        product_kernel,
        grid=(features // tile,),
        in_specs=[whole, whole, part, part],
        out_specs=pl.BlockSpec((rows, tile), lambda i: (0, i)),
        out_shape=jax.ShapeDtypeStruct((rows, features), F32),
        compiler_params=pltpu.CompilerParams(vmem_limit_bytes=32 * 2**20),
        cost_estimate=pl.CostEstimate(
            flops=4 * rows * columns * features,
            bytes_accessed=4 * columns * features + 4 * rows * (features + columns),
            transcendentals=0,
        ),
    )(*grad, *weights)


def head_kernel(*refs):
    out = refs[-1]
    n = len(refs) // 2
    total = None
    for rows, grad in zip(refs[:n], refs[n:-1]):
        part = lax.dot_general(
            rows[...], grad[...], (((0,), (0,)), ((), ())), preferred_element_type=F32
        )
        total = part if total is None else total + part
    out[...] = total


def head(rows, grads, tile=512):
    features, columns = rows[0].shape[1], grads[0].shape[1]
    return pl.pallas_call(
        head_kernel,
        grid=(features // tile,),
        in_specs=[pl.BlockSpec((r.shape[0], tile), lambda i: (0, i)) for r in rows]
        + [pl.BlockSpec(g.shape, lambda i: (0, 0)) for g in grads],
        out_specs=pl.BlockSpec((tile, columns), lambda i: (i, 0)),
        out_shape=jax.ShapeDtypeStruct((features, columns), F32),
        compiler_params=pltpu.CompilerParams(vmem_limit_bytes=32 * 2**20),
        cost_estimate=pl.CostEstimate(
            flops=4 * 1024 * columns * features // 2,
            bytes_accessed=2048 * features + 4 * columns * features,
            transcendentals=0,
        ),
    )(*rows, *grads)


def per_device(hidden_states, head_weight, targets, train_step):
    hidden = hidden_states[0]
    weight = head_weight[0]
    columns = weight.shape[1]
    vocab = lax.axis_index("vocab")
    dp = lax.axis_index("dp")
    core = vocab % 2
    share = 0.5 * jnp.minimum(train_step[0].astype(F32) / WARMUP, 1.0)
    to_local, to_global = (
        lax.dynamic_index_in_dim(jnp.asarray(t.reshape(64, 32)), core * 32 + dp, 0, keepdims=False)
        for t in row_tables()
    )

    mine = lax.dynamic_slice_in_dim(hidden, core * 16, 16, 0)
    u1, d1 = ring(mine, SMALL, 1), ring(mine, SMALL, -1)
    u2, d2 = ring(u1, SMALL, 1), ring(d1, SMALL, -1, (1,))
    near = jnp.concatenate([mine, u1, u2, d1], 0)
    up1, down1 = ring(near, LARGE, 1), ring(near, LARGE, -1)
    u3, d3 = ring(u2, SMALL, 1, (1,)), ring(d2, SMALL, -1, (1,))
    u4 = ring(u3, SMALL, 1, (1,))
    wide = jnp.concatenate([u3, u4, d2, d3], 0)
    up2 = ring(up1, LARGE, 1)
    down2 = ring(jnp.where(core == 0, down1, wide), LARGE, -1)
    up3 = ring(jnp.where(core == 0, up2, wide), LARGE, 1)
    down3 = ring(down2, LARGE, -1)

    weights = (weight, vocab_flip(weight, 1))
    ids = lax.dynamic_index_in_dim(targets.reshape(32, 2, 16), core, 1, keepdims=False)
    (ids,) = reorder(to_local, ids.reshape(4, 128))
    ids = ids.reshape(512)

    def scores(rows):
        logits = [jnp.dot(rows, w, preferred_element_type=F32) for w in weights]
        peak = jnp.maximum(*[jnp.max(part, axis=-1) for part in logits])
        exps = [jnp.exp(part - peak[:, None]) for part in logits]
        total = jnp.sum(exps[0], axis=-1) + jnp.sum(exps[1], axis=-1)
        sent = partner(jnp.concatenate([(e * PROB_SCALE).astype(F16) for e in exps], 1))
        return peak, total, exps, sent

    rows = [jnp.concatenate([near, up1, down1, up2, down2, up3], 0)]
    results = [scores(rows[0])]
    far = ring(up3, LARGE, 1, (0,))
    rows.append(jnp.concatenate([down3, jnp.where(core == 0, far, wide)], 0))
    results.append(scores(rows[1]))

    peak, total = reorder(
        to_global, *[jnp.concatenate([r[i] for r in results]).reshape(4, 128) for i in range(2)]
    )
    stat = jnp.stack([peak, total])
    stat = combine(stat, *[dp_flip(stat, k) for k in (1, 2, 3)])
    stat = combine(stat, *[dp_flip(stat, 4 * k) for k in (1, 2, 3)])
    stat = combine(stat, vocab_flip(stat, 2))
    own_factor, partner_factor = factors(
        to_local,
        share,
        stat,
        dp_flip(stat, 16),
        peak,
        partner(jnp.concatenate([stat, peak[None]], 0)),
        partner_dp_flip(stat, 16),
    )
    own_factor, partner_factor = own_factor.reshape(512), partner_factor.reshape(512)

    grads = []
    for part, (_, _, exps, sent) in zip((slice(0, BIG), slice(BIG, 512)), results):
        sides = []
        for side in range(2):
            first = (dp * 4 + (vocab ^ side)) * columns
            onehot = (first + lax.iota(jnp.int32, columns))[None, :] == ids[part][:, None]
            other = sent[:, side * columns : (side + 1) * columns].astype(F32)
            grad = exps[side] * own_factor[part][:, None] - onehot.astype(F32)
            sides.append((grad - other * partner_factor[part][:, None]).astype(BF16))
        grads.append(sides)

    last = product(grads[1], weights)
    p_down3, p_far = last[:64], last[64:]
    sent_far, held = lax.optimization_barrier((p_far.astype(F16), grads[0]))
    first = product(held, weights)
    p_near, p_up1, p_down1, p_up2, p_down2, p_up3 = (first[64 * i : 64 * i + 64] for i in range(6))

    def pass_on(value, axes, step, cores=(0, 1)):
        return ring(value.astype(F16), axes, step, cores).astype(F32)

    def only(which, value):
        return jnp.where(core == which, value, 0.0)

    c1 = ring(sent_far, LARGE, -1, (0,)).astype(F32)
    c2d = pass_on(p_down3, LARGE, 1)
    c2u = pass_on(p_up3 + c1, LARGE, -1)
    c3d = pass_on(p_down2 + c2d, LARGE, 1)
    c3u = pass_on(p_up2 + only(0, c2u), LARGE, -1)
    c4d = pass_on(p_down1 + only(0, c3d), LARGE, 1)
    c4u = pass_on(p_up1 + c3u, LARGE, -1)
    p_wide = (p_far + c2u + c3d).reshape(4, 16, 4096)
    e1 = pass_on(p_wide[1], SMALL, -1, (1,))
    e2d = pass_on(p_wide[3], SMALL, 1, (1,))
    e2u = pass_on(p_wide[0] + e1, SMALL, -1, (1,))
    e3d = pass_on(p_wide[2] + e2d, SMALL, 1, (1,))
    p_near = (p_near + c4u + c4d).reshape(4, 16, 4096)
    e3u = pass_on(p_near[2] + e2u, SMALL, -1)
    e4d = pass_on(p_near[3] + e3d, SMALL, 1)
    e4u = pass_on(p_near[1] + e3u, SMALL, -1)
    total = p_near[0] + e4u + e4d

    low, high = total[:, :2048], total[:, 2048:]
    came = vocab_flip(jnp.where(vocab < 2, high, low).astype(F16), 2).astype(F32)
    total = jnp.where(vocab < 2, low, high) + came
    low, high = total[:, :1024], total[:, 1024:]
    came = vocab_flip(jnp.where(core == 0, high, low), 1)
    grad_hidden = jnp.concatenate(
        [jnp.where(core == 0, low, came), jnp.where(core == 0, came, high)], 0
    ) * (1.0 / GRAD_SCALE)

    grad_head = head(
        rows + [vocab_flip(r, 1) for r in rows],
        [g[0] for g in grads] + [vocab_flip(g[1], 1) for g in grads],
    )
    return (grad_hidden[None], grad_head[None])


def solution(mesh):
    placed = (P("mp", "dp", None), P("mp", None, ("dp", "vocab")), P(), P())
    return jax.shard_map(
        per_device,
        mesh=mesh,
        in_specs=placed,
        out_specs=(P("mp", "dp", "vocab"), P("mp", None, ("dp", "vocab"))),
        check_vma=False,
    )
```

time: 1110 us -> 223 us (0.20)
  blocking collectives: 651 us -> 0 us
  waiting for transfers between devices: 407 us -> 53.3 us
  starting transfers between devices: 0.42 us -> 89 us
  Pallas kernels: 0 us -> 28.6 us
  other arithmetic: 4.28 us -> 20.8 us
  matrix products: 26.4 us -> 12.3 us
  between operations: 14.4 us -> 2.05 us
    psum x1 -> x0, blocking collectives: 327 us -> none  [row_log_norm(): lax.psum(jnp.sum(jnp.exp(values - row_max[..., None]), axis=-1), ('dp', '...]
    pmax x1 -> x0, blocking collectives: 324 us -> none  [row_log_norm(): row_max = lax.pmax(local_peak, ('dp', 'vocab'))]
    reduce_scatter x2 -> x0, waiting for transfers between devices: 257 us -> none  [the longest x1 236 us: per_device(): lax.psum_scatter(lax.dot_general(logit_grad, weight, (((1,), (1,)), ((),...]
    all_gather x1 -> x0, waiting for transfers between devices: 104 us -> none  [per_device(): gathered = lax.all_gather(hidden_states, 'dp', axis=1, tiled=True)[0]]
    ppermute x1 -> x47, starting transfers between devices: 0.31 us -> 89 us  [the longest x28 49.4 us: ring(): return lax.ppermute(value, ('dp', 'vocab'), pairs)]
    pallas_call x0 -> x6, Pallas kernels: none -> 28.6 us  [the longest x2 14.4 us: product(): pl.pallas_call(product_kernel, grid=(features // tile,), in_specs=[whole,...]
    dot_general x3 -> x4, matrix products: 26.4 us -> 12.3 us  [scores(): logits = [jnp.dot(rows, w, preferred_element_type=F32) for w in weights]]
    ppermute x1 -> x47, waiting for transfers between devices: 45.7 us -> 53.3 us  [the longest x28 48.3 us: ring(): return lax.ppermute(value, ('dp', 'vocab'), pairs)]
  transfers between devices with their start and end apart: 4 -> 47, of which waited for: 4 -> 16; matrix products, arithmetic and copies ran while one was open for 2% -> 13% of each run, Pallas kernels for 0% -> 12%
where the time goes in v1:
time: 223 us; the launch traced here: 221 us
  starting transfers between devices  89 us (40%)
  waiting for transfers between devices  53.3 us (24%)
  Pallas kernels  28.6 us (13%)
  other arithmetic  20.8 us (9%)
  local copies, waits for them, and re-layouts  15.4 us (7%)
  matrix products  12.3 us (6%)
    ppermute x28, starting transfers between devices, ring(): return lax.ppermute(value, ('dp', 'vocab'), pairs)  49.4 us
    ppermute x28, waiting for transfers between devices, ring(): return lax.ppermute(value, ('dp', 'vocab'), pairs)  48.3 us
    ppermute x8, starting transfers between devices, vocab_flip(): return lax.ppermute(value, 'vocab', [(v, v ^ mask) for v in range(4)])  24.6 us
    pallas_call x2, Pallas kernels, product(): pl.pallas_call(product_kernel, grid=(features // tile,), in_specs=[whole,...  14.4 us
    dot_general x4, matrix products, scores(): logits = [jnp.dot(rows, w, preferred_element_type=F32) for w in weights]  12.3 us
    ppermute x7, starting transfers between devices, dp_flip(): return lax.ppermute(value, 'dp', [(i, i ^ mask) for i in range(Z * X)])  10.6 us
    pallas_call x1, Pallas kernels, head(): pl.pallas_call(head_kernel, grid=(features // tile,), in_specs=[pl.BlockS...  9.73 us
    unnamed x62, local copies, waits for them, and re-layouts  5.89 us
  transfers between devices with their start and end apart: 47, of which 16 were waited for; matrix products, arithmetic and copies ran while one was open for 13% of the time, Pallas kernels for 12%

profile of v1, /device:TPU:1, one launch (start us, length us, event | category | flops | bytes accessed | tf_op | source)
XLA Modules:
  0.0 221.5 jit_solution(13874481143400745083)
XLA Ops:
  1.6 2.5 %collective-permute-start = (bf16[16,4096]{1,0:T(8,128)(2,1)S(1)}, bf16[16,4096]{1,0:T(8,128)(2,1)S(1)}, u32[]{:S(2)}, u32[]{:S(2)}) collective-permute-start(bf16[16,4096]{1,0:T(8,128)(2,1)S(1)} %get-tuple-element.27), channel_id=1, source_target_pairs={{0,4},{1,17},{2,6},{3,19},{4,8},{5,21},{6,10},{7,23},{8,12},{9,25}... | collective-permute-start | bytes 393224 | tf_op jit(solution)/shard_map/ppermute | solution.py:46
  4.1 4.0 %collective-permute-start.2 = (bf16[16,4096]{1,0:T(8,128)(2,1)S(1)}, bf16[16,4096]{1,0:T(8,128)(2,1)S(1)}, u32[]{:S(2)}, u32[]{:S(2)}) collective-permute-start(bf16[16,4096]{1,0:T(8,128)(2,1)S(1)} %get-tuple-element.27), channel_id=1, source_target_pairs={{0,12},{1,113},{2,14},{3,115},{4,0},{5,117},{6,2},{7,119},{8,4},{9... | collective-permute-start | bytes 393224 | tf_op jit(solution)/shard_map/ppermute | solution.py:46
  8.2 2.5 %collective-permute-done = bf16[16,4096]{1,0:T(8,128)(2,1)S(1)} collective-permute-done((bf16[16,4096]{1,0:T(8,128)(2,1)S(1)}, bf16[16,4096]{1,0:T(8,128)(2,1)S(1)}, u32[]{:S(2)}, u32[]{:S(2)}) %collective-permute-start) | collective-permute-done | bytes 131104 | tf_op jit(solution)/shard_map/ppermute | solution.py:46
  10.7 4.7 %collective-permute-start.6 = (bf16[16,4096]{1,0:T(8,128)(2,1)S(1)}, bf16[16,4096]{1,0:T(8,128)(2,1)S(1)}, u32[]{:S(2)}, u32[]{:S(2)}) collective-permute-start(bf16[16,4096]{1,0:T(8,128)(2,1)S(1)} %collective-permute-done.2), channel_id=1, source_target_pairs={{1,113},{3,115},{5,117},{7,119},{9,121},{11,123},{13,125},{15,127}... | collective-permute-start | bytes 393224 | tf_op jit(solution)/shard_map/ppermute | solution.py:46
  16.8 2.0 collective-permute-start.3
  18.8 1.9 collective-permute-start.4
  20.8 4.6 %collective-permute-start.7 = (bf16[16,4096]{1,0:T(8,128)(2,1)S(1)}, bf16[16,4096]{1,0:T(8,128)(2,1)S(1)}, u32[]{:S(2)}, u32[]{:S(2)}) collective-permute-start(bf16[16,4096]{1,0:T(8,128)(2,1)S(1)} %collective-permute-done.6), channel_id=1, source_target_pairs={{1,113},{3,115},{5,117},{7,119},{9,121},{11,123},{13,125},{15,127}... | collective-permute-start | bytes 393224 | tf_op jit(solution)/shard_map/ppermute | solution.py:46
  25.4 2.0 collective-permute-done.4
  27.4 1.9 collective-permute-start.5
  29.3 5.0 %collective-permute-done.5 = bf16[16,4096]{1,0:T(8,128)(2,1)S(1)} collective-permute-done((bf16[16,4096]{1,0:T(8,128)(2,1)S(1)}, bf16[16,4096]{1,0:T(8,128)(2,1)S(1)}, u32[]{:S(2)}, u32[]{:S(2)}) %collective-permute-start.5) | collective-permute-done | bytes 131104 | tf_op jit(solution)/shard_map/ppermute | solution.py:46
  35.4 8.4 %collective-permute-done.11 = bf16[64,4096]{1,0:T(8,128)(2,1)S(1)} collective-permute-done((bf16[64,4096]{1,0:T(8,128)(2,1)S(1)}, bf16[64,4096]{1,0:T(8,128)(2,1)S(1)}, u32[]{:S(2)}, u32[]{:S(2)}) %collective-permute-start.11) | collective-permute-done | bytes 524320 | tf_op jit(solution)/shard_map/ppermute | solution.py:46
  43.7 1.3 constant_dynamic-update-slice_fusion.6
  45.0 2.7 %collective-permute-start.8 = (bf16[64,4096]{1,0:T(8,128)(2,1)}, bf16[64,4096]{1,0:T(8,128)(2,1)}, u32[]{:S(2)}, u32[]{:S(2)}) collective-permute-start(bf16[64,4096]{1,0:T(8,128)(2,1)} %get-tuple-element.45), channel_id=1, source_target_pairs={{0,112},{1,13},{2,114},{3,15},{4,116},{5,1},{6,118},{7,3},{8,120},... | collective-permute-start | bytes 1572872 | tf_op jit(solution)/shard_map/ppermute | solution.py:46
  48.5 1.3 fusion.33.table
  49.8 1.4 shard_map.79
  51.2 1.2 fusion.34.table
  52.4 1.3 slice_bitcast_fusion.15
  55.2 2.0 collective-permute-start.9
  57.2 1.1 constant_dynamic-update-slice_fusion.5
  58.3 1.1 constant_dynamic-update-slice_fusion.4.refs_0_
  59.4 4.2 %fusion.44 = (f32[384]{0:T(512)S(1)}, f32[384,512]{1,0:T(8,128)S(1)}) fusion(bf16[384,4096]{1,0:T(8,128)(2,1)S(1)} %constant_dynamic-update-slice_fusion.4.refs_0_, bf16[1,4096,512]{2,1,0:T(8,128)(2,1)} %param.7), kind=kOutput, calls=%fused_computation.134 | convolution fusion | flops 1610808960 | bytes 8128000 | tf_op jit(solution)/shard_map/dot_general | solution.py:223
  64.9 3.1 %fusion.43 = (f32[128]{0:T(128)S(1)}, f32[128,512]{1,0:T(8,128)S(1)}) fusion(bf16[4096,512]{1,0:T(8,128)(2,1)} %collective-permute-done.14.weight_other, bf16[64,4096]{1,0:T(8,128)(2,1)S(1)} %broadcast_select_fusion, bf16[64,4096]{1,0:T(8,128)(2,1)S(1)} %collective-permute-done.9), kind=kOutput, calls=%fused_computation.133 | convolution fusion | flops 539033472 | bytes 5505536 | tf_op jit(solution)/shard_map/dot_general | solution.py:223
  68.0 4.1 %fusion.45 = (f32[384]{0:T(512)S(1)}, f32[384,512]{1,0:T(8,128)S(1)}) fusion(bf16[384,4096]{1,0:T(8,128)(2,1)S(1)} %constant_dynamic-update-slice_fusion.4.refs_0_, bf16[4096,512]{1,0:T(8,128)(2,1)} %collective-permute-done.14.weight_other), kind=kOutput, calls=%fused_computation.135 | convolution fusion | flops 1610808960 | bytes 8128000 | tf_op jit(solution)/shard_map/dot_general | solution.py:223
  73.2 1.2 fusion.9
  75.0 1.5 shard_map.77
  76.4 1.3 pad_maximum_fusion.5
  77.7 2.6 %collective-permute-start.17 = (f32[2,4,128]{2,1,0:T(4,128)}, f32[2,4,128]{2,1,0:T(4,128)S(1)}, u32[]{:S(2)}, u32[]{:S(2)}) collective-permute-start(f32[2,4,128]{2,1,0:T(4,128)} %pad_maximum_fusion.5), channel_id=1, source_target_pairs={{0,12},{4,8},{8,4},{12,0},{16,28},{20,24},{24,20},{28,16},{32,44},... | collective-permute-start | bytes 12296 | tf_op jit(solution)/shard_map/ppermute | solution.py:53
  81.0 1.2 slice_bitcast_fusion.18
  82.1 2.4 %collective-permute-done.16 = f32[2,4,128]{2,1,0:T(4,128)S(1)} collective-permute-done((f32[2,4,128]{2,1,0:T(4,128)}, f32[2,4,128]{2,1,0:T(4,128)S(1)}, u32[]{:S(2)}, u32[]{:S(2)}) %collective-permute-start.16) | collective-permute-done | bytes 4128 | tf_op jit(solution)/shard_map/ppermute | solution.py:53
  85.2 1.4 collective-permute-start.20
  86.6 2.3 %collective-permute-start.18 = (f32[2,4,128]{2,1,0:T(4,128)S(1)}, f32[2,4,128]{2,1,0:T(4,128)S(1)}, u32[]{:S(2)}, u32[]{:S(2)}) collective-permute-start(f32[2,4,128]{2,1,0:T(4,128)S(1)} %pad_maximum_fusion.6), channel_id=1, source_target_pairs={{0,16},{4,20},{8,24},{12,28},{16,0},{20,4},{24,8},{28,12},{32,48},... | collective-permute-start | bytes 12296 | tf_op jit(solution)/shard_map/ppermute | solution.py:53
  90.0 3.0 %collective-permute-start.21 = (f32[2,4,128]{2,1,0:T(4,128)S(1)}, f32[2,4,128]{2,1,0:T(4,128)S(1)}, u32[]{:S(2)}, u32[]{:S(2)}) collective-permute-start(f32[2,4,128]{2,1,0:T(4,128)S(1)} %pad_maximum_fusion.7), channel_id=1, source_target_pairs={{0,2},{1,3},{2,0},{3,1},{4,6},{5,7},{6,4},{7,5},{8,10},{9,11},{10,... | collective-permute-start | bytes 12296 | tf_op jit(solution)/shard_map/ppermute | solution.py:57
  93.0 1.7 pad_maximum_fusion.3
  95.8 3.7 %collective-permute-start.22 = (f32[2,4,128]{2,1,0:T(4,128)S(1)}, f32[2,4,128]{2,1,0:T(4,128)S(1)}, u32[]{:S(2)}, u32[]{:S(2)}) collective-permute-start(f32[2,4,128]{2,1,0:T(4,128)S(1)} %pad_maximum_fusion.8.stat), channel_id=1, source_target_pairs={{0,64},{4,68},{8,72},{12,76},{16,80},{20,84},{24,88},{28,92},{32,9... | collective-permute-start | bytes 12296 | tf_op jit(solution)/shard_map/ppermute | solution.py:53
  99.5 2.5 %collective-permute-start.24 = (f32[2,4,128]{2,1,0:T(4,128)S(1)}, f32[2,4,128]{2,1,0:T(4,128)S(1)}, u32[]{:S(2)}, u32[]{:S(2)}) collective-permute-start(f32[2,4,128]{2,1,0:T(4,128)S(1)} %pad_maximum_fusion.8.stat), channel_id=1, source_target_pairs={{0,192},{4,196},{8,200},{12,204},{16,208},{20,212},{24,216},{28,22... | collective-permute-start | bytes 12296 | tf_op jit(solution)/shard_map/ppermute | solution.py:66
  102.4 2.1 pad_maximum_fusion.1
  104.5 1.1 collective-permute-start.26
  105.5 1.3 collective-permute-done.24.p_came
  107.4 1.6 shard_map.78
  111.7 1.4 subtract_convert_fusion.2
  113.2 2.3 %copy-done.1 = bf16[1,4096,512]{2,1,0:T(8,128)(2,1)S(1)} copy-done((bf16[1,4096,512]{2,1,0:T(8,128)(2,1)S(1)}, bf16[1,4096,512]{2,1,0:T(8,128)(2,1)}, u32[]{:S(2)}) %copy-start.1) | copy-done | bytes 4194328
  115.5 6.9 %shard_map.80 = f32[128,4096]{1,0:T(8,128)S(1)} custom-call(bf16[128,512]{1,0:T(8,128)(2,1)S(1)} %get-tuple-element.47.own.refs_5_, bf16[128,512]{1,0:T(8,128)(2,1)S(1)} %get-tuple-element.46.other, bf16[4096,512]{1,0:T(8,128)(2,1)S(1)} %bitcast.152, bf16[4096,512]{1,0:T(8,128)(2,1)} %collective-permute-done.14.weight_other), custom_call_target="tpu_custom_call" | custom-call | flops 1073741824 | bytes 10747904 | tf_op jit(solution)/shard_map/pallas_call | solution.py:146
  122.5 1.9 subtract_convert_fusion
  125.2 7.6 %shard_map.81 = f32[384,4096]{1,0:T(8,128)S(1)} custom-call(bf16[384,512]{1,0:T(8,128)(2,1)S(1)} %get-tuple-element.13.own.refs_4_, bf16[384,512]{1,0:T(8,128)(2,1)S(1)} %get-tuple-element.14.other, bf16[4096,512]{1,0:T(8,128)(2,1)S(1)} %bitcast.153, bf16[4096,512]{1,0:T(8,128)(2,1)} %collective-permute-done.14.weight_other), custom_call_target="tpu_custom_call" | custom-call | flops 3221225472 | bytes 15466496 | tf_op jit(solution)/shard_map/pallas_call | solution.py:146
  134.4 6.9 %collective-permute-done.28 = f16[64,4096]{1,0:T(8,128)(2,1)S(1)} collective-permute-done((f16[64,4096]{1,0:T(8,128)(2,1)S(1)}, f16[64,4096]{1,0:T(8,128)(2,1)S(1)}, u32[]{:S(2)}, u32[]{:S(2)}) %collective-permute-start.28) | collective-permute-done | bytes 524320 | tf_op jit(solution)/shard_map/ppermute | solution.py:46
  141.5 1.4 collective-permute-start.29
  142.9 7.0 %collective-permute-done.29 = f16[64,4096]{1,0:T(8,128)(2,1)S(1)} collective-permute-done((f16[64,4096]{1,0:T(8,128)(2,1)S(1)}, f16[64,4096]{1,0:T(8,128)(2,1)S(1)}, u32[]{:S(2)}, u32[]{:S(2)}) %collective-permute-start.29) | collective-permute-done | bytes 524320 | tf_op jit(solution)/shard_map/ppermute | solution.py:46
  150.3 9.2 %collective-permute-done.32 = f16[64,4096]{1,0:T(8,128)(2,1)S(1)} collective-permute-done((f16[64,4096]{1,0:T(8,128)(2,1)S(1)}, f16[64,4096]{1,0:T(8,128)(2,1)S(1)}, u32[]{:S(2)}, u32[]{:S(2)}) %collective-permute-start.32) | collective-permute-done | bytes 524320 | tf_op jit(solution)/shard_map/ppermute | solution.py:46
  160.0 4.4 %collective-permute-start.34 = (f16[16,4096]{1,0:T(8,128)(2,1)S(1)}, f16[16,4096]{1,0:T(8,128)(2,1)S(1)}, u32[]{:S(2)}, u32[]{:S(2)}) collective-permute-start(f16[16,4096]{1,0:T(8,128)(2,1)S(1)} %get-tuple-element.40), channel_id=1, source_target_pairs={{1,113},{3,115},{5,117},{7,119},{9,121},{11,123},{13,125},{15,127}... | collective-permute-start | bytes 393224 | tf_op jit(solution)/shard_map/ppermute | solution.py:46
  164.4 1.9 collective-permute-start.38
  166.3 1.5 collective-permute-start.30
  167.9 5.2 %collective-permute-done.38 = f16[16,4096]{1,0:T(8,128)(2,1)S(1)} collective-permute-done((f16[16,4096]{1,0:T(8,128)(2,1)S(1)}, f16[16,4096]{1,0:T(8,128)(2,1)S(1)}, u32[]{:S(2)}, u32[]{:S(2)}) %collective-permute-start.38) | collective-permute-done | bytes 131104 | tf_op jit(solution)/shard_map/ppermute | solution.py:46
  173.8 1.9 collective-permute-start.35
  175.7 3.4 %collective-permute-start.39 = (f16[16,4096]{1,0:T(8,128)(2,1)}, f16[16,4096]{1,0:T(8,128)(2,1)}, u32[]{:S(2)}, u32[]{:S(2)}) collective-permute-start(f16[16,4096]{1,0:T(8,128)(2,1)} %get-tuple-element.35), channel_id=1, source_target_pairs={{1,17},{3,19},{5,21},{7,23},{9,25},{11,27},{13,29},{15,31},{17,33}... | collective-permute-start | bytes 393224 | tf_op jit(solution)/shard_map/ppermute | solution.py:46
  181.0 1.2 collective-permute-start.36
  182.2 10.6 %collective-permute-start.43 = (bf16[384,4096]{1,0:T(8,128)(2,1)S(1)}, bf16[384,4096]{1,0:T(8,128)(2,1)S(1)}, u32[]{:S(2)}, u32[]{:S(2)}) collective-permute-start(bf16[384,4096]{1,0:T(8,128)(2,1)S(1)} %constant_dynamic-update-slice_fusion.4.refs_0_), channel_id=1, source_target_pairs={{0,1},{1,0},{2,3},{3,2},{4,5},{5,4},{6,7},{7,6},{8,9},{9,8},{10,11... | collective-permute-start | bytes 9437192 | tf_op jit(solution)/shard_map/ppermute | solution.py:57
  192.8 1.2 fusion.14
  194.3 2.4 %collective-permute-start.37 = (f16[16,4096]{1,0:T(8,128)(2,1)S(1)}, f16[16,4096]{1,0:T(8,128)(2,1)S(1)}, u32[]{:S(2)}, u32[]{:S(2)}) collective-permute-start(f16[16,4096]{1,0:T(8,128)(2,1)S(1)} %get-tuple-element.32), channel_id=1, source_target_pairs={{0,12},{1,113},{2,14},{3,115},{4,0},{5,117},{6,2},{7,119},{8,4},{9... | collective-permute-start | bytes 393224 | tf_op jit(solution)/shard_map/ppermute | solution.py:46
  196.7 1.3 pad_maximum_fusion.refs_1_
  198.0 4.2 %collective-permute-start.44 = (bf16[128,4096]{1,0:T(8,128)(2,1)S(1)}, bf16[128,4096]{1,0:T(8,128)(2,1)S(1)}, u32[]{:S(2)}, u32[]{:S(2)}) collective-permute-start(bf16[128,4096]{1,0:T(8,128)(2,1)S(1)} %pad_maximum_fusion.refs_1_), channel_id=1, source_target_pairs={{0,1},{1,0},{2,3},{3,2},{4,5},{5,4},{6,7},{7,6},{8,9},{9,8},{10,11... | collective-permute-start | bytes 3145736 | tf_op jit(solution)/shard_map/ppermute | solution.py:57
  203.2 2.1 collective-permute-start.41
  205.3 1.9 collective-permute-start.46
  208.2 2.8 %collective-permute-start.42 = (f32[16,1024]{1,0:T(8,128)S(1)}, f32[16,1024]{1,0:T(8,128)S(1)}, u32[]{:S(2)}, u32[]{:S(2)}) collective-permute-start(f32[16,1024]{1,0:T(8,128)S(1)} %slice_select_fusion), channel_id=1, source_target_pairs={{0,1},{1,0},{2,3},{3,2},{4,5},{5,4},{6,7},{7,6},{8,9},{9,8},{10,11... | collective-permute-start | bytes 196616 | tf_op jit(solution)/shard_map/ppermute | solution.py:57
  211.0 9.7 %shard_map.82 = f32[4096,512]{1,0:T(8,128)} custom-call(bf16[384,4096]{1,0:T(8,128)(2,1)S(1)} %constant_dynamic-update-slice_fusion.4.refs_0_, bf16[128,4096]{1,0:T(8,128)(2,1)S(1)} %pad_maximum_fusion.refs_1_, bf16[384,4096]{1,0:T(8,128)(2,1)S(1)} %collective-permute-done.43.refs_2_, bf16[128,4096]{1,0:T(8,128)(2,1)S(1)} %collective-permute-done.44.refs_3_, ...), custom_call_target="tpu_custom_call" | custom-call | flops 4294967296 | bytes 16777216 | tf_op jit(solution)/shard_map/pallas_call | solution.py:175
  (155 shorter events, 24.3 us)
Async XLA Ops:
  1.6 9.1 %collective-permute-start = (bf16[16,4096]{1,0:T(8,128)(2,1)S(1)}, bf16[16,4096]{1,0:T(8,128)(2,1)S(1)}, u32[]{:S(2)}, u32[]{:S(2)}) collective-permute-start(bf16[16,4096]{1,0:T(8,128)(2,1)S(1)} %get-tuple-element.27), channel_id=1, source_target_pairs={{0,4},{1,17},{2,6},{3,19},{4,8},{5,21},{6,10},{7,23},{8,12},{9,25}... | collective-permute-start | bytes 393224 | tf_op jit(solution)/shard_map/ppermute | solution.py:46
  4.1 6.6 %collective-permute-start.2 = (bf16[16,4096]{1,0:T(8,128)(2,1)S(1)}, bf16[16,4096]{1,0:T(8,128)(2,1)S(1)}, u32[]{:S(2)}, u32[]{:S(2)}) collective-permute-start(bf16[16,4096]{1,0:T(8,128)(2,1)S(1)} %get-tuple-element.27), channel_id=1, source_target_pairs={{0,12},{1,113},{2,14},{3,115},{4,0},{5,117},{6,2},{7,119},{8,4},{9... | collective-permute-start | bytes 393224 | tf_op jit(solution)/shard_map/ppermute | solution.py:46
  8.2 56.7 %collective-permute-start.14 = (bf16[4096,512]{1,0:T(8,128)(2,1)}, bf16[4096,512]{1,0:T(8,128)(2,1)}, u32[]{:S(2)}, u32[]{:S(2)}) collective-permute-start(bf16[4096,512]{1,0:T(8,128)(2,1)} %bitcast.151), channel_id=1, source_target_pairs={{0,1},{1,0},{2,3},{3,2},{4,5},{5,4},{6,7},{7,6},{8,9},{9,8},{10,11... | collective-permute-start | bytes 12582920 | tf_op jit(solution)/shard_map/ppermute | solution.py:57
  10.7 5.3 %collective-permute-start.1 = (bf16[16,4096]{1,0:T(8,128)(2,1)S(1)}, bf16[16,4096]{1,0:T(8,128)(2,1)S(1)}, u32[]{:S(2)}, u32[]{:S(2)}) collective-permute-start(bf16[16,4096]{1,0:T(8,128)(2,1)S(1)} %collective-permute-done), channel_id=1, source_target_pairs={{0,4},{1,17},{2,6},{3,19},{4,8},{5,21},{6,10},{7,23},{8,12},{9,25}... | collective-permute-start | bytes 393224 | tf_op jit(solution)/shard_map/ppermute | solution.py:46
  10.7 10.1 %collective-permute-start.6 = (bf16[16,4096]{1,0:T(8,128)(2,1)S(1)}, bf16[16,4096]{1,0:T(8,128)(2,1)S(1)}, u32[]{:S(2)}, u32[]{:S(2)}) collective-permute-start(bf16[16,4096]{1,0:T(8,128)(2,1)S(1)} %collective-permute-done.2), channel_id=1, source_target_pairs={{1,113},{3,115},{5,117},{7,119},{9,121},{11,123},{13,125},{15,127}... | collective-permute-start | bytes 393224 | tf_op jit(solution)/shard_map/ppermute | solution.py:46
  16.0 18.3 %collective-permute-start.10 = (bf16[64,4096]{1,0:T(8,128)(2,1)S(1)}, bf16[64,4096]{1,0:T(8,128)(2,1)S(1)}, u32[]{:S(2)}, u32[]{:S(2)}) collective-permute-start(bf16[64,4096]{1,0:T(8,128)(2,1)S(1)} %pad_maximum_fusion.2), channel_id=1, source_target_pairs={{0,16},{1,5},{2,18},{3,7},{4,20},{5,9},{6,22},{7,11},{8,24},{9,13}... | collective-permute-start | bytes 1572872 | tf_op jit(solution)/shard_map/ppermute | solution.py:46
  16.8 18.5 %collective-permute-start.3 = (bf16[64,4096]{1,0:T(8,128)(2,1)S(1)}, bf16[64,4096]{1,0:T(8,128)(2,1)S(1)}, u32[]{:S(2)}, u32[]{:S(2)}) collective-permute-start(bf16[64,4096]{1,0:T(8,128)(2,1)S(1)} %pad_maximum_fusion.2), channel_id=1, source_target_pairs={{0,112},{1,13},{2,114},{3,15},{4,116},{5,1},{6,118},{7,3},{8,120},... | collective-permute-start | bytes 1572872 | tf_op jit(solution)/shard_map/ppermute | solution.py:46
  18.8 8.6 %collective-permute-start.4 = (bf16[16,4096]{1,0:T(8,128)(2,1)S(1)}, bf16[16,4096]{1,0:T(8,128)(2,1)S(1)}, u32[]{:S(2)}, u32[]{:S(2)}) collective-permute-start(bf16[16,4096]{1,0:T(8,128)(2,1)S(1)} %collective-permute-done.1), channel_id=1, source_target_pairs={{1,17},{3,19},{5,21},{7,23},{9,25},{11,27},{13,29},{15,31},{17,33}... | collective-permute-start | bytes 393224 | tf_op jit(solution)/shard_map/ppermute | solution.py:46
  20.8 26.9 %copy-start.23 = (s32[1024]{0:T(1024)S(1)}, s32[1024]{0:T(1024)}, u32[]{:S(2)}) copy-start(s32[1024]{0:T(1024)} %param.8) | copy-start | bytes 12292
  20.8 13.6 %collective-permute-start.7 = (bf16[16,4096]{1,0:T(8,128)(2,1)S(1)}, bf16[16,4096]{1,0:T(8,128)(2,1)S(1)}, u32[]{:S(2)}, u32[]{:S(2)}) collective-permute-start(bf16[16,4096]{1,0:T(8,128)(2,1)S(1)} %collective-permute-done.6), channel_id=1, source_target_pairs={{1,113},{3,115},{5,117},{7,119},{9,121},{11,123},{13,125},{15,127}... | collective-permute-start | bytes 393224 | tf_op jit(solution)/shard_map/ppermute | solution.py:46
  27.4 6.9 %collective-permute-start.5 = (bf16[16,4096]{1,0:T(8,128)(2,1)S(1)}, bf16[16,4096]{1,0:T(8,128)(2,1)S(1)}, u32[]{:S(2)}, u32[]{:S(2)}) collective-permute-start(bf16[16,4096]{1,0:T(8,128)(2,1)S(1)} %collective-permute-done.4), channel_id=1, source_target_pairs={{1,17},{3,19},{5,21},{7,23},{9,25},{11,27},{13,29},{15,31},{17,33}... | collective-permute-start | bytes 393224 | tf_op jit(solution)/shard_map/ppermute | solution.py:46
  34.4 10.6 %copy-start.14 = (bf16[64,4096]{1,0:T(8,128)(2,1)}, bf16[64,4096]{1,0:T(8,128)(2,1)S(1)}, u32[]{:S(2)}) copy-start(bf16[64,4096]{1,0:T(8,128)(2,1)S(1)} %constant_dynamic-update-slice_fusion) | copy-start | bytes 1572868
  34.4 9.3 %collective-permute-start.11 = (bf16[64,4096]{1,0:T(8,128)(2,1)S(1)}, bf16[64,4096]{1,0:T(8,128)(2,1)S(1)}, u32[]{:S(2)}, u32[]{:S(2)}) collective-permute-start(bf16[64,4096]{1,0:T(8,128)(2,1)S(1)} %collective-permute-done.10), channel_id=1, source_target_pairs={{0,16},{1,5},{2,18},{3,7},{4,20},{5,9},{6,22},{7,11},{8,24},{9,13}... | collective-permute-start | bytes 1572872 | tf_op jit(solution)/shard_map/ppermute | solution.py:46
  45.0 9.6 %collective-permute-start.12 = (bf16[64,4096]{1,0:T(8,128)(2,1)}, bf16[64,4096]{1,0:T(8,128)(2,1)}, u32[]{:S(2)}, u32[]{:S(2)}) collective-permute-start(bf16[64,4096]{1,0:T(8,128)(2,1)} %get-tuple-element.44), channel_id=1, source_target_pairs={{0,16},{1,5},{2,18},{3,7},{4,20},{5,9},{6,22},{7,11},{8,24},{9,13}... | collective-permute-start | bytes 1572872 | tf_op jit(solution)/shard_map/ppermute | solution.py:46
  45.0 10.2 %collective-permute-start.8 = (bf16[64,4096]{1,0:T(8,128)(2,1)}, bf16[64,4096]{1,0:T(8,128)(2,1)}, u32[]{:S(2)}, u32[]{:S(2)}) collective-permute-start(bf16[64,4096]{1,0:T(8,128)(2,1)} %get-tuple-element.45), channel_id=1, source_target_pairs={{0,112},{1,13},{2,114},{3,15},{4,116},{5,1},{6,118},{7,3},{8,120},... | collective-permute-start | bytes 1572872 | tf_op jit(solution)/shard_map/ppermute | solution.py:46
  54.5 9.1 %collective-permute-start.13 = (bf16[64,4096]{1,0:T(8,128)(2,1)}, bf16[64,4096]{1,0:T(8,128)(2,1)S(1)}, u32[]{:S(2)}, u32[]{:S(2)}) collective-permute-start(bf16[64,4096]{1,0:T(8,128)(2,1)} %collective-permute-done.12), channel_id=1, source_target_pairs={{0,16},{2,18},{4,20},{6,22},{8,24},{10,26},{12,28},{14,30},{16,32}... | collective-permute-start | bytes 1572872 | tf_op jit(solution)/shard_map/ppermute | solution.py:46
  55.2 8.8 %collective-permute-start.9 = (bf16[64,4096]{1,0:T(8,128)(2,1)}, bf16[64,4096]{1,0:T(8,128)(2,1)S(1)}, u32[]{:S(2)}, u32[]{:S(2)}) collective-permute-start(bf16[64,4096]{1,0:T(8,128)(2,1)} %collective-permute-done.8), channel_id=1, source_target_pairs={{0,112},{1,13},{2,114},{3,15},{4,116},{5,1},{6,118},{7,3},{8,120},... | collective-permute-start | bytes 1572872 | tf_op jit(solution)/shard_map/ppermute | solution.py:46
  59.4 4.6 %copy-start = (bf16[1,4096,512]{2,1,0:T(8,128)(2,1)S(1)}, bf16[1,4096,512]{2,1,0:T(8,128)(2,1)}, u32[]{:S(2)}) copy-start(bf16[1,4096,512]{2,1,0:T(8,128)(2,1)} %param.7) | copy-start | bytes 12582916
  63.6 9.5 %copy-start.10 = (f32[384,512]{1,0:T(8,128)}, f32[384,512]{1,0:T(8,128)S(1)}, u32[]{:S(2)}) copy-start(f32[384,512]{1,0:T(8,128)S(1)} %get-tuple-element.59) | copy-start | bytes 2359300
  63.7 4.3 %copy-start.16 = (bf16[64,4096]{1,0:T(8,128)(2,1)}, bf16[64,4096]{1,0:T(8,128)(2,1)S(1)}, u32[]{:S(2)}) copy-start(bf16[64,4096]{1,0:T(8,128)(2,1)S(1)} %broadcast_select_fusion) | copy-start | bytes 1572868
  64.9 7.3 %copy-start.17 = (f32[128,512]{1,0:T(8,128)}, f32[128,512]{1,0:T(8,128)S(1)}, u32[]{:S(2)}) copy-start(f32[128,512]{1,0:T(8,128)S(1)} %get-tuple-element.55) | copy-start | bytes 786436
  68.0 6.3 %copy-start.22 = (f32[128]{0:T(128)}, f32[128]{0:T(128)S(1)}, u32[]{:S(2)}) copy-start(f32[128]{0:T(128)S(1)} %max.35) | copy-start | bytes 1540
  77.7 4.4 %collective-permute-start.17 = (f32[2,4,128]{2,1,0:T(4,128)}, f32[2,4,128]{2,1,0:T(4,128)S(1)}, u32[]{:S(2)}, u32[]{:S(2)}) collective-permute-start(f32[2,4,128]{2,1,0:T(4,128)} %pad_maximum_fusion.5), channel_id=1, source_target_pairs={{0,12},{4,8},{8,4},{12,0},{16,28},{20,24},{24,20},{28,16},{32,44},... | collective-permute-start | bytes 12296 | tf_op jit(solution)/shard_map/ppermute | solution.py:53
  80.3 4.2 %collective-permute-start.16 = (f32[2,4,128]{2,1,0:T(4,128)}, f32[2,4,128]{2,1,0:T(4,128)S(1)}, u32[]{:S(2)}, u32[]{:S(2)}) collective-permute-start(f32[2,4,128]{2,1,0:T(4,128)} %pad_maximum_fusion.5), channel_id=1, source_target_pairs={{0,8},{4,12},{8,0},{12,4},{16,24},{20,28},{24,16},{28,20},{32,40},... | collective-permute-start | bytes 12296 | tf_op jit(solution)/shard_map/ppermute | solution.py:53
  80.3 4.2 %collective-permute-start.15 = (f32[2,4,128]{2,1,0:T(4,128)}, f32[2,4,128]{2,1,0:T(4,128)S(1)}, u32[]{:S(2)}, u32[]{:S(2)}) collective-permute-start(f32[2,4,128]{2,1,0:T(4,128)} %pad_maximum_fusion.5), channel_id=1, source_target_pairs={{0,4},{4,0},{8,12},{12,8},{16,20},{20,16},{24,28},{28,24},{32,36},... | collective-permute-start | bytes 12296 | tf_op jit(solution)/shard_map/ppermute | solution.py:53
  85.2 4.3 %collective-permute-start.20 = (f32[2,4,128]{2,1,0:T(4,128)S(1)}, f32[2,4,128]{2,1,0:T(4,128)S(1)}, u32[]{:S(2)}, u32[]{:S(2)}) collective-permute-start(f32[2,4,128]{2,1,0:T(4,128)S(1)} %pad_maximum_fusion.6), channel_id=1, source_target_pairs={{0,48},{4,52},{8,56},{12,60},{16,32},{20,36},{24,40},{28,44},{32,1... | collective-permute-start | bytes 12296 | tf_op jit(solution)/shard_map/ppermute | solution.py:53
  86.6 3.4 %collective-permute-start.19 = (f32[2,4,128]{2,1,0:T(4,128)S(1)}, f32[2,4,128]{2,1,0:T(4,128)S(1)}, u32[]{:S(2)}, u32[]{:S(2)}) collective-permute-start(f32[2,4,128]{2,1,0:T(4,128)S(1)} %pad_maximum_fusion.6), channel_id=1, source_target_pairs={{0,32},{4,36},{8,40},{12,44},{16,48},{20,52},{24,56},{28,60},{32,0... | collective-permute-start | bytes 12296 | tf_op jit(solution)/shard_map/ppermute | solution.py:53
  86.6 3.4 %collective-permute-start.18 = (f32[2,4,128]{2,1,0:T(4,128)S(1)}, f32[2,4,128]{2,1,0:T(4,128)S(1)}, u32[]{:S(2)}, u32[]{:S(2)}) collective-permute-start(f32[2,4,128]{2,1,0:T(4,128)S(1)} %pad_maximum_fusion.6), channel_id=1, source_target_pairs={{0,16},{4,20},{8,24},{12,28},{16,0},{20,4},{24,8},{28,12},{32,48},... | collective-permute-start | bytes 12296 | tf_op jit(solution)/shard_map/ppermute | solution.py:53
  90.0 5.1 %collective-permute-start.21 = (f32[2,4,128]{2,1,0:T(4,128)S(1)}, f32[2,4,128]{2,1,0:T(4,128)S(1)}, u32[]{:S(2)}, u32[]{:S(2)}) collective-permute-start(f32[2,4,128]{2,1,0:T(4,128)S(1)} %pad_maximum_fusion.7), channel_id=1, source_target_pairs={{0,2},{1,3},{2,0},{3,1},{4,6},{5,7},{6,4},{7,5},{8,10},{9,11},{10,... | collective-permute-start | bytes 12296 | tf_op jit(solution)/shard_map/ppermute | solution.py:57
  94.7 17.0 %collective-permute-start.25 = (f16[128,1024]{1,0:T(8,128)(2,1)}, f16[128,1024]{1,0:T(8,128)(2,1)}, u32[]{:S(2)}, u32[]{:S(2)}) collective-permute-start(f16[128,1024]{1,0:T(8,128)(2,1)} %pad_maximum_fusion.3), channel_id=1, source_target_pairs={{0,128},{128,0},{1,129},{129,1},{2,130},{130,2},{3,131},{131,3},{4... | collective-permute-start | bytes 786440 | tf_op jit(solution)/shard_map/ppermute | solution.py:61
  95.2 12.2 %copy-start.20 = (f32[2,4,128]{2,1,0:T(4,128)}, f32[2,4,128]{2,1,0:T(4,128)S(1)}, u32[]{:S(2)}) copy-start(f32[2,4,128]{2,1,0:T(4,128)S(1)} %pad_maximum_fusion.8.stat) | copy-start | bytes 12292
  95.8 9.7 %collective-permute-start.22 = (f32[2,4,128]{2,1,0:T(4,128)S(1)}, f32[2,4,128]{2,1,0:T(4,128)S(1)}, u32[]{:S(2)}, u32[]{:S(2)}) collective-permute-start(f32[2,4,128]{2,1,0:T(4,128)S(1)} %pad_maximum_fusion.8.stat), channel_id=1, source_target_pairs={{0,64},{4,68},{8,72},{12,76},{16,80},{20,84},{24,88},{28,92},{32,9... | collective-permute-start | bytes 12296 | tf_op jit(solution)/shard_map/ppermute | solution.py:53
  99.5 7.3 %collective-permute-start.24 = (f32[2,4,128]{2,1,0:T(4,128)S(1)}, f32[2,4,128]{2,1,0:T(4,128)S(1)}, u32[]{:S(2)}, u32[]{:S(2)}) collective-permute-start(f32[2,4,128]{2,1,0:T(4,128)S(1)} %pad_maximum_fusion.8.stat), channel_id=1, source_target_pairs={{0,192},{4,196},{8,200},{12,204},{16,208},{20,212},{24,216},{28,22... | collective-permute-start | bytes 12296 | tf_op jit(solution)/shard_map/ppermute | solution.py:66
  102.0 5.4 %collective-permute-start.23 = (f32[3,4,128]{2,1,0:T(4,128)S(1)}, f32[3,4,128]{2,1,0:T(4,128)}, u32[]{:S(2)}, u32[]{:S(2)}) collective-permute-start(f32[3,4,128]{2,1,0:T(4,128)S(1)} %pad_maximum_fusion.4), channel_id=1, source_target_pairs={{0,128},{128,0},{1,129},{129,1},{2,130},{130,2},{3,131},{131,3},{4... | collective-permute-start | bytes 18440 | tf_op jit(solution)/shard_map/ppermute | solution.py:61
  104.5 18.0 %collective-permute-start.26 = (f16[384,1024]{1,0:T(8,128)(2,1)}, f16[384,1024]{1,0:T(8,128)(2,1)}, u32[]{:S(2)}, u32[]{:S(2)}) collective-permute-start(f16[384,1024]{1,0:T(8,128)(2,1)} %pad_maximum_fusion.1), channel_id=1, source_target_pairs={{0,128},{128,0},{1,129},{129,1},{2,130},{130,2},{3,131},{131,3},{4... | collective-permute-start | bytes 2359304 | tf_op jit(solution)/shard_map/ppermute | solution.py:61
  113.2 9.2 %copy-start.5 = (bf16[128,512]{1,0:T(8,128)(2,1)}, bf16[128,512]{1,0:T(8,128)(2,1)S(1)}, u32[]{:S(2)}) copy-start(bf16[128,512]{1,0:T(8,128)(2,1)S(1)} %get-tuple-element.47.own.refs_5_) | copy-start | bytes 393220
  113.2 9.2 %copy-start.7 = (bf16[128,512]{1,0:T(8,128)(2,1)}, bf16[128,512]{1,0:T(8,128)(2,1)S(1)}, u32[]{:S(2)}) copy-start(bf16[128,512]{1,0:T(8,128)(2,1)S(1)} %get-tuple-element.46.other) | copy-start | bytes 393220
  115.5 7.1 %copy-start.11 = (f32[384,512]{1,0:T(8,128)S(1)}, f32[384,512]{1,0:T(8,128)}, u32[]{:S(2)}) copy-start(f32[384,512]{1,0:T(8,128)} %copy-done.10) | copy-start | bytes 2359300
  115.5 7.1 %copy-start.13 = (f32[384,512]{1,0:T(8,128)S(1)}, f32[384,512]{1,0:T(8,128)}, u32[]{:S(2)}) copy-start(f32[384,512]{1,0:T(8,128)} %copy-done.12) | copy-start | bytes 2359300
  115.5 7.1 %copy-start.21 = (s32[384]{0:T(512)S(1)}, s32[384]{0:T(512)}, u32[]{:S(2)}) copy-start(s32[384]{0:T(512)} %slice_bitcast_fusion.15) | copy-start | bytes 4612
  124.4 8.3 %copy-start.3 = (bf16[384,512]{1,0:T(8,128)(2,1)}, bf16[384,512]{1,0:T(8,128)(2,1)S(1)}, u32[]{:S(2)}) copy-start(bf16[384,512]{1,0:T(8,128)(2,1)S(1)} %get-tuple-element.14.other) | copy-start | bytes 1179652
  124.4 8.3 %collective-permute-start.27 = (f16[64,4096]{1,0:T(8,128)(2,1)S(1)}, f16[64,4096]{1,0:T(8,128)(2,1)S(1)}, u32[]{:S(2)}, u32[]{:S(2)}) collective-permute-start(f16[64,4096]{1,0:T(8,128)(2,1)S(1)} %get-tuple-element.15), channel_id=1, source_target_pairs={{0,112},{2,114},{4,116},{6,118},{8,120},{10,122},{12,124},{14,126}... | collective-permute-start | bytes 1572872 | tf_op jit(solution)/shard_map/ppermute | solution.py:46
  132.9 8.4 %collective-permute-start.28 = (f16[64,4096]{1,0:T(8,128)(2,1)S(1)}, f16[64,4096]{1,0:T(8,128)(2,1)S(1)}, u32[]{:S(2)}, u32[]{:S(2)}) collective-permute-start(f16[64,4096]{1,0:T(8,128)(2,1)S(1)} %fusion.5), channel_id=1, source_target_pairs={{0,112},{1,13},{2,114},{3,15},{4,116},{5,1},{6,118},{7,3},{8,120},... | collective-permute-start | bytes 1572872 | tf_op jit(solution)/shard_map/ppermute | solution.py:46
  133.4 9.5 %collective-permute-start.31 = (f16[64,4096]{1,0:T(8,128)(2,1)S(1)}, f16[64,4096]{1,0:T(8,128)(2,1)S(1)}, u32[]{:S(2)}, u32[]{:S(2)}) collective-permute-start(f16[64,4096]{1,0:T(8,128)(2,1)S(1)} %get-tuple-element.30), channel_id=1, source_target_pairs={{0,16},{1,5},{2,18},{3,7},{4,20},{5,9},{6,22},{7,11},{8,24},{9,13}... | collective-permute-start | bytes 1572872 | tf_op jit(solution)/shard_map/ppermute | solution.py:46
  141.5 8.4 %collective-permute-start.29 = (f16[64,4096]{1,0:T(8,128)(2,1)S(1)}, f16[64,4096]{1,0:T(8,128)(2,1)S(1)}, u32[]{:S(2)}, u32[]{:S(2)}) collective-permute-start(f16[64,4096]{1,0:T(8,128)(2,1)S(1)} %fusion.1), channel_id=1, source_target_pairs={{0,112},{1,13},{2,114},{3,15},{4,116},{5,1},{6,118},{7,3},{8,120},... | collective-permute-start | bytes 1572872 | tf_op jit(solution)/shard_map/ppermute | solution.py:46
  150.2 9.3 %collective-permute-start.32 = (f16[64,4096]{1,0:T(8,128)(2,1)S(1)}, f16[64,4096]{1,0:T(8,128)(2,1)S(1)}, u32[]{:S(2)}, u32[]{:S(2)}) collective-permute-start(f16[64,4096]{1,0:T(8,128)(2,1)S(1)} %get-tuple-element.29), channel_id=1, source_target_pairs={{0,16},{1,5},{2,18},{3,7},{4,20},{5,9},{6,22},{7,11},{8,24},{9,13}... | collective-permute-start | bytes 1572872 | tf_op jit(solution)/shard_map/ppermute | solution.py:46
  160.0 7.9 %collective-permute-start.34 = (f16[16,4096]{1,0:T(8,128)(2,1)S(1)}, f16[16,4096]{1,0:T(8,128)(2,1)S(1)}, u32[]{:S(2)}, u32[]{:S(2)}) collective-permute-start(f16[16,4096]{1,0:T(8,128)(2,1)S(1)} %get-tuple-element.40), channel_id=1, source_target_pairs={{1,113},{3,115},{5,117},{7,119},{9,121},{11,123},{13,125},{15,127}... | collective-permute-start | bytes 393224 | tf_op jit(solution)/shard_map/ppermute | solution.py:46
  164.4 8.7 %collective-permute-start.38 = (f16[16,4096]{1,0:T(8,128)(2,1)S(1)}, f16[16,4096]{1,0:T(8,128)(2,1)S(1)}, u32[]{:S(2)}, u32[]{:S(2)}) collective-permute-start(f16[16,4096]{1,0:T(8,128)(2,1)S(1)} %get-tuple-element.41), channel_id=1, source_target_pairs={{1,17},{3,19},{5,21},{7,23},{9,25},{11,27},{13,29},{15,31},{17,33}... | collective-permute-start | bytes 393224 | tf_op jit(solution)/shard_map/ppermute | solution.py:46
  166.3 12.8 %collective-permute-start.30 = (f16[64,4096]{1,0:T(8,128)(2,1)S(1)}, f16[64,4096]{1,0:T(8,128)(2,1)S(1)}, u32[]{:S(2)}, u32[]{:S(2)}) collective-permute-start(f16[64,4096]{1,0:T(8,128)(2,1)S(1)} %get-tuple-element.28), channel_id=1, source_target_pairs={{0,112},{1,13},{2,114},{3,15},{4,116},{5,1},{6,118},{7,3},{8,120},... | collective-permute-start | bytes 1572872 | tf_op jit(solution)/shard_map/ppermute | solution.py:46
  167.9 11.2 %collective-permute-start.33 = (f16[64,4096]{1,0:T(8,128)(2,1)S(1)}, f16[64,4096]{1,0:T(8,128)(2,1)S(1)}, u32[]{:S(2)}, u32[]{:S(2)}) collective-permute-start(f16[64,4096]{1,0:T(8,128)(2,1)S(1)} %get-tuple-element.42), channel_id=1, source_target_pairs={{0,16},{1,5},{2,18},{3,7},{4,20},{5,9},{6,22},{7,11},{8,24},{9,13}... | collective-permute-start | bytes 1572872 | tf_op jit(solution)/shard_map/ppermute | solution.py:46
  173.8 5.7 %collective-permute-start.35 = (f16[16,4096]{1,0:T(8,128)(2,1)S(1)}, f16[16,4096]{1,0:T(8,128)(2,1)S(1)}, u32[]{:S(2)}, u32[]{:S(2)}) collective-permute-start(f16[16,4096]{1,0:T(8,128)(2,1)S(1)} %get-tuple-element.34), channel_id=1, source_target_pairs={{1,113},{3,115},{5,117},{7,119},{9,121},{11,123},{13,125},{15,127}... | collective-permute-start | bytes 393224 | tf_op jit(solution)/shard_map/ppermute | solution.py:46
  175.7 17.0 %collective-permute-start.39 = (f16[16,4096]{1,0:T(8,128)(2,1)}, f16[16,4096]{1,0:T(8,128)(2,1)}, u32[]{:S(2)}, u32[]{:S(2)}) collective-permute-start(f16[16,4096]{1,0:T(8,128)(2,1)} %get-tuple-element.35), channel_id=1, source_target_pairs={{1,17},{3,19},{5,21},{7,23},{9,25},{11,27},{13,29},{15,31},{17,33}... | collective-permute-start | bytes 393224 | tf_op jit(solution)/shard_map/ppermute | solution.py:46
  181.0 11.8 %collective-permute-start.36 = (f16[16,4096]{1,0:T(8,128)(2,1)}, f16[16,4096]{1,0:T(8,128)(2,1)}, u32[]{:S(2)}, u32[]{:S(2)}) collective-permute-start(f16[16,4096]{1,0:T(8,128)(2,1)} %fusion.13), channel_id=1, source_target_pairs={{0,12},{1,113},{2,14},{3,115},{4,0},{5,117},{6,2},{7,119},{8,4},{9... | collective-permute-start | bytes 393224 | tf_op jit(solution)/shard_map/ppermute | solution.py:46
  182.2 23.1 %copy-start.8 = (bf16[128,512]{1,0:T(8,128)(2,1)S(1)}, bf16[128,512]{1,0:T(8,128)(2,1)}, u32[]{:S(2)}) copy-start(bf16[128,512]{1,0:T(8,128)(2,1)} %copy-done.7) | copy-start | bytes 393220
  182.2 25.0 %copy-start.4 = (bf16[384,512]{1,0:T(8,128)(2,1)S(1)}, bf16[384,512]{1,0:T(8,128)(2,1)}, u32[]{:S(2)}) copy-start(bf16[384,512]{1,0:T(8,128)(2,1)} %copy-done.3) | copy-start | bytes 1179652
  182.2 28.8 %copy-start.6 = (bf16[128,512]{1,0:T(8,128)(2,1)S(1)}, bf16[128,512]{1,0:T(8,128)(2,1)}, u32[]{:S(2)}) copy-start(bf16[128,512]{1,0:T(8,128)(2,1)} %copy-done.5) | copy-start | bytes 393220
  182.2 28.8 %collective-permute-start.43 = (bf16[384,4096]{1,0:T(8,128)(2,1)S(1)}, bf16[384,4096]{1,0:T(8,128)(2,1)S(1)}, u32[]{:S(2)}, u32[]{:S(2)}) collective-permute-start(bf16[384,4096]{1,0:T(8,128)(2,1)S(1)} %constant_dynamic-update-slice_fusion.4.refs_0_), channel_id=1, source_target_pairs={{0,1},{1,0},{2,3},{3,2},{4,5},{5,4},{6,7},{7,6},{8,9},{9,8},{10,11... | collective-permute-start | bytes 9437192 | tf_op jit(solution)/shard_map/ppermute | solution.py:57
  193.9 8.2 %collective-permute-start.40 = (f16[16,4096]{1,0:T(8,128)(2,1)S(1)}, f16[16,4096]{1,0:T(8,128)(2,1)S(1)}, u32[]{:S(2)}, u32[]{:S(2)}) collective-permute-start(f16[16,4096]{1,0:T(8,128)(2,1)S(1)} %get-tuple-element.33), channel_id=1, source_target_pairs={{0,4},{1,17},{2,6},{3,19},{4,8},{5,21},{6,10},{7,23},{8,12},{9,25}... | collective-permute-start | bytes 393224 | tf_op jit(solution)/shard_map/ppermute | solution.py:46
  194.3 7.9 %collective-permute-start.37 = (f16[16,4096]{1,0:T(8,128)(2,1)S(1)}, f16[16,4096]{1,0:T(8,128)(2,1)S(1)}, u32[]{:S(2)}, u32[]{:S(2)}) collective-permute-start(f16[16,4096]{1,0:T(8,128)(2,1)S(1)} %get-tuple-element.32), channel_id=1, source_target_pairs={{0,12},{1,113},{2,14},{3,115},{4,0},{5,117},{6,2},{7,119},{8,4},{9... | collective-permute-start | bytes 393224 | tf_op jit(solution)/shard_map/ppermute | solution.py:46
  198.0 13.0 %collective-permute-start.44 = (bf16[128,4096]{1,0:T(8,128)(2,1)S(1)}, bf16[128,4096]{1,0:T(8,128)(2,1)S(1)}, u32[]{:S(2)}, u32[]{:S(2)}) collective-permute-start(bf16[128,4096]{1,0:T(8,128)(2,1)S(1)} %pad_maximum_fusion.refs_1_), channel_id=1, source_target_pairs={{0,1},{1,0},{2,3},{3,2},{4,5},{5,4},{6,7},{7,6},{8,9},{9,8},{10,11... | collective-permute-start | bytes 3145736 | tf_op jit(solution)/shard_map/ppermute | solution.py:57
  203.2 5.0 %collective-permute-start.41 = (f16[16,2048]{1,0:T(8,128)(2,1)S(1)}, f16[16,2048]{1,0:T(8,128)(2,1)S(1)}, u32[]{:S(2)}, u32[]{:S(2)}) collective-permute-start(f16[16,2048]{1,0:T(8,128)(2,1)S(1)} %select_convert_fusion), channel_id=1, source_target_pairs={{0,2},{1,3},{2,0},{3,1},{4,6},{5,7},{6,4},{7,5},{8,10},{9,11},{10,... | collective-permute-start | bytes 196616 | tf_op jit(solution)/shard_map/ppermute | solution.py:57
  205.3 5.7 %collective-permute-start.46 = (bf16[128,512]{1,0:T(8,128)(2,1)S(1)}, bf16[128,512]{1,0:T(8,128)(2,1)S(1)}, u32[]{:S(2)}, u32[]{:S(2)}) collective-permute-start(bf16[128,512]{1,0:T(8,128)(2,1)S(1)} %copy-done.8), channel_id=1, source_target_pairs={{0,1},{1,0},{2,3},{3,2},{4,5},{5,4},{6,7},{7,6},{8,9},{9,8},{10,11... | collective-permute-start | bytes 393224 | tf_op jit(solution)/shard_map/ppermute | solution.py:57
  207.2 3.8 %collective-permute-start.45 = (bf16[384,512]{1,0:T(8,128)(2,1)S(1)}, bf16[384,512]{1,0:T(8,128)(2,1)S(1)}, u32[]{:S(2)}, u32[]{:S(2)}) collective-permute-start(bf16[384,512]{1,0:T(8,128)(2,1)S(1)} %copy-done.4), channel_id=1, source_target_pairs={{0,1},{1,0},{2,3},{3,2},{4,5},{5,4},{6,7},{7,6},{8,9},{9,8},{10,11... | collective-permute-start | bytes 1179656 | tf_op jit(solution)/shard_map/ppermute | solution.py:57
  208.2 12.6 %collective-permute-start.42 = (f32[16,1024]{1,0:T(8,128)S(1)}, f32[16,1024]{1,0:T(8,128)S(1)}, u32[]{:S(2)}, u32[]{:S(2)}) collective-permute-start(f32[16,1024]{1,0:T(8,128)S(1)} %slice_select_fusion), channel_id=1, source_target_pairs={{0,1},{1,0},{2,3},{3,2},{4,5},{5,4},{6,7},{7,6},{8,9},{9,8},{10,11... | collective-permute-start | bytes 196616 | tf_op jit(solution)/shard_map/ppermute | solution.py:57
  (9 other events, 22.5 us)
